TPU v7x, 32 devices: a whole 2x2x4 slice. The times are simulated.
32 devices in a mesh: groups: 2 (over y), mp: 4 (over z), role: 2 (over core), rep: 2 (over x).
Axes of the slice: x: 2, y: 2, z: 4, core: 2. Of those that a mesh axis runs over, the one named last changes fastest.
Arguments:
- teacher_rows: bfloat16 [5120, 8192], P(('groups', 'mp', 'role'), 'rep'), parts along dimension 0, may hold values from -1400 to 1400
- teacher_gain: float32 [8192], P('rep'), may hold values from 0.5 to 2
- teacher_value: bfloat16 [8192, 1024], P('rep', 'role'), may hold values from -0.0625 to 0.0625
- student_rows: bfloat16 [10240, 5120], P(('groups', 'mp', 'role'), 'rep'), parts along dimension 0, may hold values from -1400 to 1400
- student_gain: float32 [5120], P('rep'), may hold values from 0.5 to 2
- student_value: bfloat16 [5120, 1024], P('rep', 'role'), may hold values from -0.078125 to 0.078125
- owners: int32 [5120, 1], P(('groups', 'mp', 'role')), parts along dimension 0, may hold values from 0 to 7; in each aligned block of 320 rows (0 to 319, 320 to 639, ...) at most 80 rows name the same one
Outputs:
- value_error: bfloat16 [10240, 1024], P(('groups', 'mp', 'role'), 'rep'), parts along dimension 0
- grad_value: float32 [10240, 1024], P(('groups', 'rep'), 'role'), parts along dimension 0
There are 2 independent parts, one for each index of `groups`. A program takes and returns all parts, laid end to end along the dimension named above; an argument that names none is the same for every part. Nothing has to cross between parts.
Inputs may be any that keep to these rules, and one draw needn't show every extreme that they name: `owners`: in each aligned block of 320 rows (the rows of one index of mp and role), no student shard is named by more than 80 rows, a bound that some block reaches.
All inputs are finite; a program needn't handle non-finite values.
Results may differ from a plain program's by a relative error of at most 0.012.
Values may be sent and summed in bfloat16 or wider, within the bound.
A program may use at most 128 MiB of HBM per device.

v0:
```python
import math

import jax
import jax.numpy as jnp
from jax import lax
from jax.sharding import PartitionSpec as P

DT = 8192
DS = 5120
KV = 1024


EPS = 1e-06


def squares_of(rows_in):
    widened = rows_in.astype(jnp.float32)
    return jnp.sum(widened * widened, axis=1)


def shards(
    teacher_rows, teacher_gain, teacher_value, student_rows, student_gain, student_value, owners
):
    peer_count = lax.axis_size(("mp", "role"))
    block_rows = teacher_rows.shape[0]
    slot_cap = student_rows.shape[0] // peer_count
    teacher_full, student_full = (
        lax.all_gather(teacher_value, "role", axis=1, tiled=True),
        lax.all_gather(student_value, "role", axis=1, tiled=True),
    )
    teacher_gated = (teacher_rows.astype(jnp.float32) * teacher_gain[None, :]).astype(jnp.bfloat16)
    student_gated = (student_rows.astype(jnp.float32) * student_gain[None, :]).astype(jnp.bfloat16)
    teacher_squares, student_squares = lax.psum(
        (squares_of(teacher_rows), squares_of(student_rows)), "rep"
    )
    teacher_scale = lax.rsqrt(teacher_squares / DT + EPS)
    student_scale = lax.rsqrt(student_squares / DS + EPS)
    teacher_part = jnp.dot(teacher_gated, teacher_full, preferred_element_type=jnp.float32)
    student_part = jnp.dot(student_gated, student_full, preferred_element_type=jnp.float32)
    teacher_sum, student_sum = (
        lax.psum_scatter(teacher_part, "rep", scatter_dimension=1, tiled=True),
        lax.psum_scatter(student_part, "rep", scatter_dimension=1, tiled=True),
    )
    teacher_values = (teacher_sum * teacher_scale[:, None]).astype(jnp.bfloat16)
    student_values = student_sum * student_scale[:, None]
    owner_col = owners[:, 0]
    all_owners = lax.all_gather(owner_col, ("mp", "role"), axis=0, tiled=True).reshape(
        peer_count, block_rows
    )
    myself = lax.axis_index(("mp", "role"))
    is_mine = (all_owners == myself).astype(jnp.int32)
    counts = jnp.sum(is_mine, axis=1)
    live_slot = (jnp.arange(slot_cap, dtype=jnp.int32)[None, :] < counts[:, None]).reshape(-1)
    every_row = lax.all_gather(teacher_values, ("mp", "role"), axis=0, tiled=True)
    rank_in = jnp.cumsum(is_mine, axis=1) - is_mine
    blocks = jnp.arange(peer_count, dtype=jnp.int32)[:, None]
    where_to = jnp.where(is_mine > 0, blocks * slot_cap + rank_in, peer_count * slot_cap)
    source = blocks * block_rows + jnp.arange(block_rows, dtype=jnp.int32)[None, :]
    pick_rows = (
        jnp.zeros((peer_count * slot_cap,), jnp.int32)
        .at[where_to.reshape(-1)]
        .set(source.reshape(-1), mode="drop")
    )
    target = jnp.take(every_row, pick_rows, axis=0)
    value_gap = jnp.where(live_slot[:, None], student_values - target.astype(jnp.float32), 0.0)
    value_error = value_gap.astype(jnp.bfloat16)
    tokens = peer_count * block_rows
    cotangent = (value_gap * student_scale[:, None] * (1.0 / math.sqrt(tokens))).astype(
        jnp.bfloat16
    )
    cotangent_full = lax.all_gather(cotangent, "rep", axis=1, tiled=True)
    half_cols = KV // lax.axis_size("role")
    role_index = lax.axis_index("role")
    grad_part = lax.dot_general(
        student_gated, cotangent_full, (((0,), (0,)), ((), ())), preferred_element_type=jnp.float32
    )
    grad_total = lax.psum(grad_part.astype(jnp.bfloat16), ("mp", "role")).astype(jnp.float32)
    grad_value = lax.dynamic_slice_in_dim(grad_total, role_index * half_cols, half_cols, 1)
    return (value_error, grad_value)


def solution(mesh):
    return jax.shard_map(
        shards,
        mesh=mesh,
        in_specs=(
            P(("groups", "mp", "role"), "rep"),
            P("rep"),
            P("rep", "role"),
            P(("groups", "mp", "role"), "rep"),
            P("rep"),
            P("rep", "role"),
            P(("groups", "mp", "role"), None),
        ),
        out_specs=(P(("groups", "mp", "role"), "rep"), P(("groups", "rep"), "role")),
        check_vma=False,
    )
```

profile of v0, /device:TPU:0, one launch (start us, length us, event | category | flops | bytes accessed | tf_op | source)
XLA Modules:
  0.0 321.1 jit_solution(9134642454245292030)
XLA Ops:
  7.2 0.7 all-gather.8.cloned.1.call-update
  8.0 24.2 %all-gather.8.cloned.1.call-done = bf16[4096,1024]{1,0:T(8,128)(2,1)} async-done(((bf16[4096,512]{1,0:T(8,128)(2,1)}), bf16[4096,1024]{1,0:T(8,128)(2,1)}) %all-gather.8.cloned.1.call-update) | async-done | bytes 8388624 | tf_op jit(solution)/shard_map/all_gather | solution.py:28
  32.2 7.3 %fusion.7 = f32[320,1024]{1,0:T(8,128)} fusion(bf16[4096,1024]{1,0:T(8,128)(2,1)} %all-gather.8.cloned.1.call-done, bf16[320,4096]{1,0:T(8,128)(2,1)S(1)} %copy-done.1, f32[4096]{0:T(1024)S(1)} %copy-done.3), kind=kOutput, calls=%fused_computation.12 | convolution fusion | flops 2688286720 | bytes 12337152 | tf_op jit(solution)/shard_map/dot_general | solution.py:38
  39.5 0.7 all-gather.6.cloned.1.call-update
  40.3 2.5 fusion.3
  42.8 0.7 fusion.1
  43.5 5.0 %all-reduce.2 = (f32[640]{0:T(1024)S(1)}, f32[320]{0:T(512)S(1)}) all-reduce(f32[640]{0:T(1024)S(1)} %fusion.1, f32[320]{0:T(512)S(1)} %fusion.3), channel_id=1, replica_groups=mesh['groups'=2,'mp'=4,'role'=2,'rep'=2] {'rep'}, use_global_device_ids=true, to_apply=%region_3.0 | all-reduce | flops 960 | bytes 7680 | tf_op jit(solution)/shard_map/psum | solution.py:33
  48.5 15.5 %reduce-scatter.5.cloned.1.call-done = f32[320,512]{1,0:T(8,128)} async-done(((f32[320,1024]{1,0:T(8,128)}), f32[320,512]{1,0:T(8,128)}) %reduce-scatter.5.cloned.1.call-update) | async-done | bytes 655376 | tf_op jit(solution)/shard_map/reduce_scatter | solution.py:41
  64.0 1.9 multiply_convert_fusion.1
  66.0 15.0 %all-gather.6.cloned.1.call-done = bf16[2560,1024]{1,0:T(8,128)(2,1)} async-done(((bf16[2560,512]{1,0:T(8,128)(2,1)}), bf16[2560,1024]{1,0:T(8,128)(2,1)}) %all-gather.6.cloned.1.call-update) | async-done | bytes 5242896 | tf_op jit(solution)/shard_map/all_gather | solution.py:29
  81.1 7.5 %fusion.5 = f32[640,1024]{1,0:T(8,128)} fusion(bf16[2560,1024]{1,0:T(8,128)(2,1)} %all-gather.6.cloned.1.call-done, bf16[640,2560]{1,0:T(8,128)(2,1)S(1)} %copy-done, f32[2560]{0:T(1024)S(1)} %copy-done.4), kind=kOutput, calls=%fused_computation.11 | convolution fusion | flops 3360358400 | bytes 11151360 | tf_op jit(solution)/shard_map/dot_general | solution.py:39
  88.8 0.6 dynamic-slice
  90.1 0.3 dynamic-update-slice
  90.4 30.1 %all-reduce.1 = s32[2560]{0:T(1024)S(1)} all-reduce(s32[2560]{0:T(1024)S(1)} %dynamic-update-slice), channel_id=2, replica_groups=mesh['groups'=2,'mp'=4,'role'=2,'rep'=2] {'mp','role'}, use_global_device_ids=true, to_apply=%add.1 | all-reduce | flops 2560 | bytes 20480
  120.6 0.8 reduce-window.6
  122.2 9.9 %scatter_custom_fusion = s32[640]{0:T(1024)S(1)} fusion(s32[2560]{0:T(1024)S(1)} %fusion.13, s32[2560]{0:T(1024)S(1)} %reshape.104, s32[]{:T(128)} %constant.22.clone.1), kind=kCustom, calls=%fused_computation.36 | custom fusion | bytes 2564 | tf_op jit(solution)/shard_map/scatter | solution.py:62
  132.2 5.4 %gather_fusion = bf16[640,512]{1,0:T(8,128)(2,1)} fusion(bf16[2560,512]{1,0:T(8,128)(2,1)} %all-gather.10.cloned.1.call-done, s32[1024]{0:T(1024)S(1)} %pad_clamp_fusion), kind=kCustom, calls=%fused_computation | custom fusion | bytes 1313280 | tf_op jit(solution)/shard_map/jit(_take)/gather | solution.py:64
  137.6 20.7 %reduce-scatter.3.cloned.1.call-done = f32[640,512]{1,0:T(8,128)} async-done(((f32[640,1024]{1,0:T(8,128)}), f32[640,512]{1,0:T(8,128)}) %reduce-scatter.3.cloned.1.call-update) | async-done | bytes 1310736 | tf_op jit(solution)/shard_map/reduce_scatter | solution.py:42
  158.2 3.0 multiply_convert_fusion
  161.2 0.2 all-reduce.5.cloned.1.call-start
  161.5 24.2 %all-gather.12.cloned.1.call-done = bf16[640,1024]{1,0:T(8,128)(2,1)} async-done(((bf16[640,512]{1,0:T(8,128)(2,1)}), bf16[640,1024]{1,0:T(8,128)(2,1)}) %all-gather.12.cloned.1.call-update) | async-done | bytes 1310736 | tf_op jit(solution)/shard_map/all_gather | solution.py:71
  185.6 7.3 %convolution_convert_fusion = bf16[2560,1024]{1,0:T(8,128)(2,1)} fusion(bf16[640,1024]{1,0:T(8,128)(2,1)} %all-gather.12.cloned.1.call-done, bf16[640,2560]{1,0:T(8,128)(2,1)S(1)} %copy-done, f32[2560]{0:T(1024)S(1)} %copy-done.4), kind=kOutput, calls=%fused_computation.8 | convolution fusion | flops 3362979840 | bytes 9840640 | tf_op jit(solution)/shard_map/dot_general | solution.py:74
  193.0 116.4 %all-reduce.5.cloned.1.call-done = bf16[2560,1024]{1,0:T(8,128)(2,1)} async-done(((bf16[2560,1024]{1,0:T(8,128)(2,1)}), bf16[2560,1024]{1,0:T(8,128)(2,1)}) %all-reduce.5.cloned.1.call-update) | async-done | bytes 5242896 | tf_op jit(solution)/shard_map/psum | solution.py:77
  309.4 4.8 %dynamic-slice_convert_fusion = f32[2560,512]{1,0:T(8,128)} fusion(bf16[2560,1024]{1,0:T(8,128)(2,1)} %all-reduce.5.cloned.1.call-done, s32[]{:T(128)S(6)} %select_n.35), kind=kLoop, calls=%fused_computation.13 | loop fusion | flops 1310720 | bytes 7864324 | tf_op jit(solution)/shard_map/convert_element_type | solution.py:77
  (46 shorter events, 1.4 us)
Async XLA Ops:
  7.2 25.0 %copy-start.1 = (bf16[320,4096]{1,0:T(8,128)(2,1)S(1)}, bf16[320,4096]{1,0:T(8,128)(2,1)}, u32[]{:S(2)}) copy-start(bf16[320,4096]{1,0:T(8,128)(2,1)} %param.7) | copy-start | bytes 7864324
  7.2 25.0 %copy-start.3 = (f32[4096]{0:T(1024)S(1)}, f32[4096]{0:T(1024)}, u32[]{:S(2)}) copy-start(f32[4096]{0:T(1024)} %param.8) | copy-start | bytes 49156
  7.2 25.0 %all-gather.8.cloned.1.call-start = ((), (), s32[]{:S(2)}) async-start(), calls=%async_computation.4 | async-start | bytes 12582912 | tf_op jit(solution)/shard_map/all_gather | solution.py:28
  7.9 56.1 %reduce-scatter.5.cloned.1.call-start = ((), (), s32[]{:S(2)}) async-start(), calls=%async_computation.5 | async-start | bytes 1966080 | tf_op jit(solution)/shard_map/reduce_scatter | solution.py:41
  39.5 3.4 %copy-start = (bf16[640,2560]{1,0:T(8,128)(2,1)S(1)}, bf16[640,2560]{1,0:T(8,128)(2,1)}, u32[]{:S(2)}) copy-start(bf16[640,2560]{1,0:T(8,128)(2,1)} %param.10) | copy-start | bytes 9830404
  39.5 41.6 %all-gather.6.cloned.1.call-start = ((), (), s32[]{:S(2)}) async-start(), calls=%async_computation.2 | async-start | bytes 7864320 | tf_op jit(solution)/shard_map/all_gather | solution.py:29
  40.2 40.8 %copy-start.4 = (f32[2560]{0:T(1024)S(1)}, f32[2560]{0:T(1024)}, u32[]{:S(2)}) copy-start(f32[2560]{0:T(1024)} %param.11) | copy-start | bytes 30724
  40.2 91.9 %all-gather.10.cloned.1.call-start = ((), (), s32[]{:S(2)}) async-start(), calls=%async_computation.6 | async-start | bytes 2949120 | tf_op jit(solution)/shard_map/all_gather | solution.py:54
  66.0 22.9 %copy-start.5 = (u32[32]{0:T(128)S(1)}, u32[32]{0:T(128)}, u32[]{:S(2)}) copy-start(u32[32]{0:T(128)} %constant.62) | copy-start | bytes 388
  66.0 24.1 %copy-start.2 = (s32[320,1]{0,1:T(1,128)S(1)}, s32[320,1]{0,1:T(1,128)}, u32[]{:S(2)}) copy-start(s32[320,1]{0,1:T(1,128)} %param.13) | copy-start | bytes 3844
  66.0 92.3 %reduce-scatter.3.cloned.1.call-start = ((), (), s32[]{:S(2)}) async-start(), calls=%async_computation.3 | async-start | bytes 3932160 | tf_op jit(solution)/shard_map/reduce_scatter | solution.py:42
  88.6 97.0 %all-gather.12.cloned.1.call-start = ((), (), s32[]{:S(2)}) async-start(), calls=%async_computation.7 | async-start | bytes 1966080 | tf_op jit(solution)/shard_map/all_gather | solution.py:71
  161.2 148.2 %all-reduce.5.cloned.1.call-start = ((), (), s32[]{:S(2)}) async-start(), calls=%async_computation.8 | async-start | bytes 10485760 | tf_op jit(solution)/shard_map/psum | solution.py:77
Sparse Core Ops, SparseCore 0:
  9.6 22.5 all-gather.7
  39.6 24.3 reduce-scatter.4
  65.6 15.3 all-gather.5
  83.2 35.6 all-gather.9
  121.7 36.5 reduce-scatter.2
  161.3 24.2 all-gather.11
  193.1 116.2 all-reduce.4
where the time goes:
time: 322 us; the launch traced here: 321 us
  waiting for transfers between devices  217 us (67%)
  blocking collectives  35.1 us (11%)
  matrix products  22.1 us (7%)
  local copies, waits for them, and re-layouts  16.8 us (5%)
  between operations  14.9 us (5%)
  other arithmetic  14.3 us (4%)
    psum x1, waiting for transfers between devices, shards(): lax.psum(grad_part.astype(jnp.bfloat16), ('mp', 'role')).astype(jnp.float32)  116 us
    unnamed x1, blocking collectives  30.1 us
    all_gather x1, waiting for transfers between devices, shards(): lax.all_gather(teacher_value, 'role', axis=1, tiled=True)  24.2 us
    all_gather x1, waiting for transfers between devices, shards(): cotangent_full = lax.all_gather(cotangent, 'rep', axis=1, tiled=True)  24.2 us
    reduce_scatter x1, waiting for transfers between devices, shards(): lax.psum_scatter(student_part, 'rep', scatter_dimension=1, tiled=True)  20.7 us
    reduce_scatter x1, waiting for transfers between devices, shards(): lax.psum_scatter(teacher_part, 'rep', scatter_dimension=1, tiled=True)  15.5 us
    all_gather x1, waiting for transfers between devices, shards(): lax.all_gather(student_value, 'role', axis=1, tiled=True)  15 us
    scatter x1, local copies, waits for them, and re-layouts, shards(): pick_rows = jnp.zeros((peer_count * slot_cap,), jnp.int32).at[where_to.re...  9.91 us
  transfers between devices with their start and end apart: 7, of which 6 were waited for; matrix products, arithmetic and copies ran while one was open for 10% of the time, Pallas kernels for 0%

commit v1 on v0

--- a/solution.py
+++ b/solution.py
@@ -3,6 +3,8 @@
 import jax
 import jax.numpy as jnp
 from jax import lax
+from jax.experimental import pallas as pl
+from jax.experimental.pallas import tpu as pltpu
 from jax.sharding import PartitionSpec as P
 
 DT = 8192
@@ -79,9 +81,410 @@
     return (value_error, grad_value)
 
 
+MESH = pl.DeviceIdType.MESH
+SENTINEL = 1048576.0
+
+
+def fused(
+    t_hbm, tg_ref, tw_hbm, s_hbm, sg_ref, sw_hbm, ow_ref,
+    err_ref, grad_ref,
+    tr, sr, tw, sw, ow, gt, tp, sp, tsq, ssq, tx_out, tx_in, sx_out, sx_in,
+    tq_out, tq_in, sq_out, sq_in, pk, tgt, gap, gap_half, cot, part_out, outer_in, mid_in,
+    lsem, sib_s, sib_r, x_s, x_r, q_s, q_r, z_s, z_r, g_s, g_r, v_s, v_r,
+    a_s, a_r, b_s, b_r, c_s, c_r,
+):
+    g, m = lax.axis_index("groups"), lax.axis_index("mp")
+    r, x = lax.axis_index("role"), lax.axis_index("rep")
+    blk, tk = t_hbm.shape
+    slots, sk = s_hbm.shape
+    cols = tw_hbm.shape[1]
+    half = cols // 2
+    n_mp = lax.axis_size("mp")
+    cap = slots // (2 * n_mp)
+    tokens = blk * 2 * n_mp
+    sib = (g, m, 1 - r, x)
+    xp = (g, m, r, 1 - x)
+
+    def z_dev(k):
+        return (g, lax.rem(m + k, n_mp), r, x)
+
+    peers = [sib, xp] + [z_dev(k) for k in range(1, n_mp)]
+    barrier = pltpu.get_barrier_semaphore()
+    for d in peers:
+        pl.semaphore_signal(barrier, inc=1, device_id=d, device_id_type=MESH)
+
+    loc = [
+        pltpu.make_async_copy(t_hbm, tr.at[r], lsem.at[0]),
+        pltpu.make_async_copy(tw_hbm, tw, lsem.at[1]),
+        pltpu.make_async_copy(s_hbm, sr.at[r], lsem.at[2]),
+        pltpu.make_async_copy(sw_hbm, sw, lsem.at[3]),
+        pltpu.make_async_copy(ow_ref, ow.at[r], lsem.at[4]),
+    ]
+    for c in loc:
+        c.start()
+    pl.semaphore_wait(barrier, len(peers))
+
+    def remote(src, dst, ss, rs, dev):
+        return pltpu.make_async_remote_copy(
+            src_ref=src, dst_ref=dst, send_sem=ss, recv_sem=rs, device_id=dev, device_id_type=MESH
+        )
+
+    sib_t = remote(t_hbm, tr.at[r], sib_s.at[0], sib_r.at[0], sib)
+    sib_o = remote(ow_ref, ow.at[r], sib_s.at[1], sib_r.at[1], sib)
+    sib_x = remote(s_hbm, sr.at[r], sib_s.at[2], sib_r.at[2], sib)
+    sib_t.start()
+    sib_o.start()
+    sib_x.start()
+
+    keep = pl.ds(pl.multiple_of(x * half, half), half)
+    give = pl.ds(pl.multiple_of((1 - x) * half, half), half)
+
+    def square_lanes(v):
+        v = v * v
+        total = v[:, 0:128]
+        for j in range(1, v.shape[1] // 128):
+            total = total + v[:, j * 128 : (j + 1) * 128]
+        return total
+
+    rt = 64
+
+    def project(src, b, dst, out, gain, w, sq, depth, kt):
+        rows = src.shape[1]
+        sq[...] = jnp.zeros_like(sq)
+        out[...] = jnp.zeros_like(out)
+
+        @pl.loop(0, depth // kt)
+        def _(k):
+            ks = pl.ds(pl.multiple_of(k * kt, kt), kt)
+            gain_k = gain[:, ks]
+
+            @pl.loop(0, rows // rt)
+            def _(i):
+                rs = pl.ds(pl.multiple_of(i * rt, rt), rt)
+                v = src[b, rs, ks].astype(jnp.float32)
+                sq[rs, :] += square_lanes(v)
+                if dst is None:
+                    src[b, rs, ks] = (v * gain_k).astype(jnp.bfloat16)
+                else:
+                    dst[rs, :] = (v * gain_k).astype(jnp.bfloat16)
+
+            gated = src[b, :, ks] if dst is None else dst[...]
+            out[...] += jnp.dot(gated, w[ks, :], preferred_element_type=jnp.float32)
+
+    def send_half(out, stage_out, stage_in, sq, q_out, q_in, slot):
+        stage_out[slot] = out[:, give].astype(jnp.bfloat16)
+        q_out[slot] = jnp.broadcast_to(
+            jnp.sum(sq[...].T, axis=0, keepdims=True), q_out.shape[1:]
+        )
+        return stage_out, q_out
+
+    def x_pair(stage_out, stage_in, q_out, q_in, slot, n):
+        return (
+            remote(stage_out.at[slot], stage_in.at[slot], x_s.at[n], x_r.at[n], xp),
+            remote(q_out.at[slot], q_in.at[slot], q_s.at[n], q_r.at[n], xp),
+        )
+
+    t_copies = []
+    for step in range(2):
+        b = r if step == 0 else 1 - r
+        if step == 0:
+            loc[0].wait()
+            loc[1].wait()
+        else:
+            sib_t.wait_recv()
+        project(tr, b, gt, tp.at[step], tg_ref, tw, tsq, tk, 512)
+        send_half(tp.at[step], tx_out, tx_in, tsq, tq_out, tq_in, step)
+        pair = x_pair(tx_out, tx_in, tq_out, tq_in, step, step)
+        for c in pair:
+            c.start()
+        t_copies.append(pair)
+
+    s_copies = []
+
+    def student(step):
+        b = r if step == 0 else 1 - r
+        if step == 0:
+            loc[2].wait()
+            loc[3].wait()
+        else:
+            sib_x.wait_recv()
+        project(sr, b, None, sp.at[step], sg_ref, sw, ssq, sk, 512)
+        send_half(sp.at[step], sx_out, sx_in, ssq, sq_out, sq_in, step)
+        pair = x_pair(sx_out, sx_in, sq_out, sq_in, step, 2 + step)
+        for c in pair:
+            c.start()
+        s_copies.append(pair)
+
+    def column(row):
+        n = row.shape[1]
+        return jnp.broadcast_to(row, (128, n)).T
+
+    student(0)
+    loc[4].wait()
+    sib_o.wait_recv()
+    n_own = 2 * n_mp
+    wide = ow.shape[2]
+    for step in range(2):
+        for c in t_copies[step]:
+            c.wait_recv()
+        b = r if step == 0 else 1 - r
+        sq_sum = tq_out[step, 0:1, :] + tq_in[step, 0:1, :]
+        scale = column(lax.rsqrt(sq_sum / DT + EPS))[0:blk]
+        scale = jnp.concatenate([scale] * (half // 128), axis=1)
+        values = tp[step, :, keep] + tx_in[step].astype(jnp.float32)
+        values = (values * scale).astype(jnp.bfloat16)
+        own = ow[b]
+        eq = (own == lax.broadcasted_iota(jnp.int32, (8, wide), 0)).astype(jnp.float32)
+        upper = (
+            lax.broadcasted_iota(jnp.int32, (wide, wide), 0)
+            < lax.broadcasted_iota(jnp.int32, (wide, wide), 1)
+        ).astype(jnp.float32)
+        before = jnp.dot(
+            eq.astype(jnp.bfloat16), upper.astype(jnp.bfloat16), preferred_element_type=jnp.float32
+        )
+        rank = jnp.sum(eq * before, axis=0, keepdims=True)
+        dest = own[0:1, :].astype(jnp.float32) * cap + rank
+        for o in range(n_own // 2):
+            spot = lax.broadcasted_iota(jnp.int32, (2 * cap, wide), 0) + o * 2 * cap
+            hit = (spot.astype(jnp.float32) == dest).astype(jnp.float32)
+            filled = jnp.sum(hit, axis=1, keepdims=True)
+            moved = jnp.dot(
+                hit[:, 0:blk].astype(jnp.bfloat16), values, preferred_element_type=jnp.float32
+            )
+            moved = jnp.where(filled > 0.5, moved, SENTINEL).astype(jnp.bfloat16)
+            pk[2 * o, b] = moved[0:cap]
+            pk[2 * o + 1, b] = moved[cap:]
+    z_copies = []
+    for k in range(1, n_mp):
+        to = lax.rem(m + k, n_mp)
+        c = remote(pk.at[pl.ds(2 * to, 2)], tgt.at[:, m], z_s.at[k - 1], z_r.at[k - 1], z_dev(k))
+        c.start()
+        z_copies.append(c)
+    tgt[0, m] = pk[2 * m]
+    tgt[1, m] = pk[2 * m + 1]
+
+    student(1)
+    for step in range(2):
+        for c in s_copies[step]:
+            c.wait_recv()
+    for c in z_copies:
+        c.wait_recv()
+
+    norm = 1.0 / math.sqrt(tokens)
+    gap_copies = []
+    for step in range(2):
+        b = r if step == 0 else 1 - r
+        sq_sum = sq_out[step, 0:1, :] + sq_in[step, 0:1, :]
+        scale = column(lax.rsqrt(sq_sum / DS + EPS))
+        per = 2 * cap
+        for s in range(n_mp):
+            rs = slice(s * per, (s + 1) * per)
+            sc = jnp.concatenate([scale[rs]] * (half // 128), axis=1)
+            vals = (sp[step, rs, keep] + sx_in[step, rs].astype(jnp.float32)) * sc
+            target = tgt[b, s].reshape(per, half).astype(jnp.float32)
+            diff = jnp.where(target < 0.5 * SENTINEL, vals - target, 0.0)
+            gap_half[b, rs] = diff.astype(jnp.bfloat16)
+            cot[b, rs] = (diff * sc * norm).astype(jnp.bfloat16)
+        c = remote(gap_half.at[b], gap.at[b], g_s.at[step], g_r.at[step], xp)
+        c.start()
+        gap_copies.append(c)
+        sp[step, :, 0:128] = scale
+
+    fb = 256
+    n_f = sk // fb
+    outer = (m == 0) | (m == n_mp - 1)
+    inward = jnp.where(m < n_mp // 2, m + 1, m - 1)
+    outward = jnp.where(m < n_mp // 2, m - 1, m + 1)
+    near = (g, jnp.where(outer, inward, outward), r, x)
+    across = (g, inward, r, x)
+    n_c = 2 * n_f
+
+    def up(i):
+        return remote(part_out.at[i], outer_in.at[i], a_s.at[i], a_r.at[i], near)
+
+    def cross(i):
+        return remote(part_out.at[i], mid_in.at[i], b_s.at[i], b_r.at[i], across)
+
+    def place(i):
+        f = lax.rem(i, n_f)
+        h = jnp.where(i < n_f, x, 1 - x)
+        return (
+            pl.ds(pl.multiple_of(f * fb, fb), fb),
+            pl.ds(pl.multiple_of(h * half, half), half),
+        )
+
+    def down(i):
+        spot = grad_ref.at[place(i)]
+        return remote(spot, spot, c_s.at[i], c_r.at[i], near)
+
+    def grad_part(i):
+        f = lax.rem(i, n_f)
+        fs = pl.ds(pl.multiple_of(f * fb, fb), fb)
+        total = None
+        for b in range(2):
+            term = lax.dot_general(
+                sr[b, :, fs], cot[b], (((0,), (0,)), ((), ())), preferred_element_type=jnp.float32
+            )
+            total = term if total is None else total + term
+        return total
+
+    def finish(i):
+        cross(i).wait_recv()
+        both = part_out[i].astype(jnp.float32) + mid_in[i].astype(jnp.float32)
+        grad_ref[place(i)] = both.astype(jnp.bfloat16)
+        down(i).start()
+
+    def chunk(i):
+        mine = grad_part(i)
+
+        @pl.when(outer)
+        def _():
+            part_out[i] = mine.astype(jnp.bfloat16)
+            up(i).start()
+
+        @pl.when(jnp.logical_not(outer))
+        def _():
+            up(i).wait_recv()
+            part_out[i] = (mine + outer_in[i].astype(jnp.float32)).astype(jnp.bfloat16)
+            cross(i).start()
+
+            @pl.when(i > 0)
+            def _():
+                finish(i - 1)
+
+    def error_copy(n):
+        src, spot = (gap_half, keep) if n == 0 else (gap, give)
+        return remote(src.at[1 - r], err_ref.at[:, spot], v_s.at[n], v_r.at[n], sib)
+
+    pl.loop(0, n_f)(chunk)
+    for step in range(2):
+        b = r if step == 0 else 1 - r
+        gap_copies[step].wait_recv()
+        sc = jnp.concatenate([sp[step, :, 0:128]] * (half // 128), axis=1)
+        cot[b] = (gap[b].astype(jnp.float32) * sc * norm).astype(jnp.bfloat16)
+
+    @pl.when(r == x)
+    def _():
+        error_copy(0).start()
+        error_copy(1).start()
+        err_ref[:, keep] = gap_half[r]
+        err_ref[:, give] = gap[r]
+
+    pl.loop(n_f, n_c)(chunk)
+
+    @pl.when(outer)
+    def _():
+        @pl.loop(0, n_c)
+        def _(i):
+            down(i).wait_recv()
+            up(i).wait_send()
+
+    @pl.when(jnp.logical_not(outer))
+    def _():
+        finish(n_c - 1)
+
+        @pl.loop(0, n_c)
+        def _(i):
+            cross(i).wait_send()
+            down(i).wait_send()
+
+    @pl.when(r == x)
+    def _():
+        error_copy(0).wait_send()
+        error_copy(1).wait_send()
+
+    @pl.when(r != x)
+    def _():
+        error_copy(0).wait_recv()
+        error_copy(1).wait_recv()
+
+    for c in [sib_t, sib_o, sib_x] + z_copies + gap_copies:
+        c.wait_send()
+    for pair in t_copies + s_copies:
+        for c in pair:
+            c.wait_send()
+
+
+def shards_fused(
+    teacher_rows, teacher_gain, teacher_value, student_rows, student_gain, student_value, owners
+):
+    blk, tk = teacher_rows.shape
+    slots, sk = student_rows.shape
+    cols = teacher_value.shape[1]
+    half = cols // 2
+    n_mp = lax.axis_size("mp")
+    cap = slots // (2 * n_mp)
+    wide = -(-blk // 128) * 128
+    own = jnp.pad(owners[:, 0], (0, wide - blk), constant_values=-1)
+    own = jnp.broadcast_to(own[None, :], (8, wide))
+    n_c = 2 * (sk // 256)
+    bf, f32, vmem, dma = jnp.bfloat16, jnp.float32, pltpu.VMEM, pltpu.SemaphoreType.DMA
+    hbm = pl.BlockSpec(memory_space=pl.ANY)
+    inv = pl.BlockSpec(memory_space=vmem)
+    scratch = [
+        vmem((2, blk, tk), bf),
+        vmem((2, slots, sk), bf),
+        vmem((tk, cols), bf),
+        vmem((sk, cols), bf),
+        vmem((2, 8, wide), jnp.int32),
+        vmem((blk, 512), bf),
+        vmem((2, blk, cols), f32),
+        vmem((2, slots, cols), f32),
+        vmem((wide, 128), f32),
+        vmem((slots, 128), f32),
+        vmem((2, blk, half), bf),
+        vmem((2, blk, half), bf),
+        vmem((2, slots, half), bf),
+        vmem((2, slots, half), bf),
+        vmem((2, 8, wide), f32),
+        vmem((2, 8, wide), f32),
+        vmem((2, 8, slots), f32),
+        vmem((2, 8, slots), f32),
+        vmem((2 * n_mp, 2, cap, half), bf),
+        vmem((2, n_mp, 2, cap, half), bf),
+        vmem((2, slots, half), bf),
+        vmem((2, slots, half), bf),
+        vmem((2, slots, half), bf),
+        vmem((n_c, 256, half), bf),
+        vmem((n_c, 256, half), bf),
+        vmem((n_c, 256, half), bf),
+        dma((5,)),
+        dma((3,)), dma((3,)),
+        dma((4,)), dma((4,)),
+        dma((4,)), dma((4,)),
+        dma((3,)), dma((3,)),
+        dma((2,)), dma((2,)),
+        dma((2,)), dma((2,)),
+        dma((n_c,)), dma((n_c,)),
+        dma((n_c,)), dma((n_c,)),
+        dma((n_c,)), dma((n_c,)),
+    ]
+    err, grad = pl.pallas_call(
+        fused,
+        out_shape=(
+            jax.ShapeDtypeStruct((slots, cols), bf),
+            jax.ShapeDtypeStruct((sk, cols), bf),
+        ),
+        in_specs=[hbm, inv, hbm, hbm, inv, hbm, hbm],
+        out_specs=(inv, inv),
+        scratch_shapes=scratch,
+        compiler_params=pltpu.CompilerParams(
+            collective_id=1, has_side_effects=True, vmem_limit_bytes=58 * 2**20
+        ),
+        cost_estimate=pl.CostEstimate(
+            flops=10 * 10**9, bytes_accessed=20 * 10**6, transcendentals=0
+        ),
+    )(
+        teacher_rows, teacher_gain[None, :], teacher_value,
+        student_rows, student_gain[None, :], student_value, own,
+    )
+    return err, grad.astype(f32)
+
+
 def solution(mesh):
+    sizes = (mesh.shape["mp"], mesh.shape["role"], mesh.shape["rep"])
     return jax.shard_map(
-        shards,
+        shards_fused if sizes == (4, 2, 2) else shards,
         mesh=mesh,
         in_specs=(
             P(("groups", "mp", "role"), "rep"),

time: 322 us -> 118 us (0.37)
  waiting for transfers between devices: 217 us -> 0 us
  Pallas kernels: 0 us -> 109 us
  blocking collectives: 35.1 us -> 0 us
  matrix products: 22.1 us -> 0 us
  between operations: 14.9 us -> 0.65 us
  local copies, waits for them, and re-layouts: 16.8 us -> 2.76 us
  other arithmetic: 14.3 us -> 5.61 us
    psum x1 -> x0, waiting for transfers between devices: 116 us -> none  [shards(): lax.psum(grad_part.astype(jnp.bfloat16), ('mp', 'role')).astype(jnp.float32)]
    pallas_call x0 -> x1, Pallas kernels: none -> 109 us  [shards_fused(): pl.pallas_call(fused, out_shape=(jax.ShapeDtypeStruct((slots, cols), bf),...]
    all_gather x4 -> x0, waiting for transfers between devices: 63.4 us -> none  [the longest x1 24.2 us: shards(): lax.all_gather(teacher_value, 'role', axis=1, tiled=True)]
    reduce_scatter x2 -> x0, waiting for transfers between devices: 36.1 us -> none  [the longest x1 20.7 us: shards(): lax.psum_scatter(student_part, 'rep', scatter_dimension=1, tiled=True)]
    unnamed x1 -> x0, blocking collectives: 30.1 us -> none
    dot_general x3 -> x0, matrix products: 22.1 us -> none  [the longest x1 7.52 us: shards(): jnp.dot(student_gated, student_full, preferred_element_type=jnp.float32)]
    scatter x1 -> x0, local copies, waits for them, and re-layouts: 9.91 us -> none  [shards(): pick_rows = jnp.zeros((peer_count * slot_cap,), jnp.int32).at[where_to.re...]
    gather x1 -> x0, local copies, waits for them, and re-layouts: 5.39 us -> none  [shards(): target = jnp.take(every_row, pick_rows, axis=0)]
  transfers between devices with their start and end apart: 7 -> 0, of which waited for: 6 -> 0; matrix products, arithmetic and copies ran while one was open for 10% -> 0% of each run, Pallas kernels for 0% -> 0%
where the time goes in v1:
time: 118 us
  Pallas kernels  109 us (92%)
  other arithmetic  5.61 us (5%)
  local copies, waits for them, and re-layouts  2.76 us (2%)
    pallas_call x1, Pallas kernels, shards_fused(): pl.pallas_call(fused, out_shape=(jax.ShapeDtypeStruct((slots, cols), bf),...  109 us
    convert_element_type x1, other arithmetic, shards_fused(): return (err, grad.astype(f32))  4.91 us

profile of v1, /device:TPU:0, one launch (start us, length us, event | category | flops | bytes accessed | tf_op | source)
XLA Modules:
  0.0 117.8 jit_solution(4874056604418600396)
XLA Ops:
  0.6 0.7 reduce
  1.3 0.6 broadcast_in_dim.14.ow_ref
  1.9 1.3 %broadcast_in_dim.13.sg_ref = f32[1,2560]{1,0:T(1,128)} reshape(f32[2560]{0:T(1024)} %param.11) | data formatting | bytes 20480 | tf_op jit(solution)/shard_map/broadcast_in_dim | solution.py:479
  3.3 108.7 %shard_map.86 = (bf16[640,512]{1,0:T(8,128)(2,1)}, bf16[2560,512]{1,0:T(8,128)(2,1)}) custom-call(bf16[320,4096]{1,0:T(8,128)(2,1)} %t_hbm.1, f32[1,4096]{1,0:T(1,128)} %bitcast.1, bf16[4096,512]{1,0:T(8,128)(2,1)} %tw_hbm.1, bf16[640,2560]{1,0:T(8,128)(2,1)} %s_hbm.1, f32[1,2560]{1,0:T(1,128)} %broadcast_in_dim.13.sg_ref, bf16[2560,512]{1,0:T(8,128)(2,1)} %sw_hbm.1, ...), custom_call_target="tpu_custom_call" | custom-call | flops 10000000000 | bytes 20000000 | tf_op jit(solution)/shard_map/pallas_call | solution.py:462
  112.0 0.0 copy-start
  112.0 4.9 %convert_element_type.3 = f32[2560,512]{1,0:T(8,128)} convert(bf16[2560,512]{1,0:T(8,128)(2,1)} %get-tuple-element.5) | non-fusion elementwise | flops 1310720 | bytes 7864320 | tf_op jit(solution)/shard_map/convert_element_type | solution.py:481
  116.9 0.0 copy-done
  116.9 0.8 copy.10
  (1 shorter events, 0.0 us)
Async XLA Ops:
  112.0 4.9 %copy-start = (bf16[640,512]{1,0:T(8,128)(2,1)S(1)}, bf16[640,512]{1,0:T(8,128)(2,1)}, u32[]{:S(2)}) copy-start(bf16[640,512]{1,0:T(8,128)(2,1)} %get-tuple-element.8) | copy-start | bytes 1966084

commit v2 on v1

--- a/solution.py
+++ b/solution.py
@@ -88,8 +88,8 @@
 def fused(
     t_hbm, tg_ref, tw_hbm, s_hbm, sg_ref, sw_hbm, ow_ref,
     err_ref, grad_ref,
-    tr, sr, tw, sw, ow, gt, tp, sp, tsq, ssq, tx_out, tx_in, sx_out, sx_in,
-    tq_out, tq_in, sq_out, sq_in, pk, tgt, gap, gap_half, cot, part_out, outer_in, mid_in,
+    tr, sr, tw, sw, ow, srt, tp, sp, tsq, ssq, tx_out, tx_in, sx_out, sx_in,
+    tq_out, tq_in, sq_out, sq_in, pk, tgt, gap, gap_half, cot, sc_ref, part_out, outer_in, mid_in,
     lsem, sib_s, sib_r, x_s, x_r, q_s, q_r, z_s, z_r, g_s, g_r, v_s, v_r,
     a_s, a_r, b_s, b_r, c_s, c_r,
 ):
@@ -102,6 +102,8 @@
     n_mp = lax.axis_size("mp")
     cap = slots // (2 * n_mp)
     tokens = blk * 2 * n_mp
+    fb = 256
+    n_f = sk // fb
     sib = (g, m, 1 - r, x)
     xp = (g, m, r, 1 - x)
 
@@ -118,10 +120,12 @@
         pltpu.make_async_copy(tw_hbm, tw, lsem.at[1]),
         pltpu.make_async_copy(s_hbm, sr.at[r], lsem.at[2]),
         pltpu.make_async_copy(sw_hbm, sw, lsem.at[3]),
-        pltpu.make_async_copy(ow_ref, ow.at[r], lsem.at[4]),
     ]
-    for c in loc:
-        c.start()
+    for n in (0, 1):
+        loc[n].start()
+    wide = ow.shape[2]
+    ow[r] = jnp.full((8, wide), -1.0, jnp.float32)
+    ow[r, :, 0:blk] = jnp.broadcast_to(ow_ref[...].astype(jnp.float32), (8, blk))
     pl.semaphore_wait(barrier, len(peers))
 
     def remote(src, dst, ss, rs, dev):
@@ -130,53 +134,40 @@
         )
 
     sib_t = remote(t_hbm, tr.at[r], sib_s.at[0], sib_r.at[0], sib)
-    sib_o = remote(ow_ref, ow.at[r], sib_s.at[1], sib_r.at[1], sib)
+    sib_o = remote(ow.at[r], ow.at[r], sib_s.at[1], sib_r.at[1], sib)
     sib_x = remote(s_hbm, sr.at[r], sib_s.at[2], sib_r.at[2], sib)
     sib_t.start()
     sib_o.start()
-    sib_x.start()
 
     keep = pl.ds(pl.multiple_of(x * half, half), half)
     give = pl.ds(pl.multiple_of((1 - x) * half, half), half)
 
-    def square_lanes(v):
-        v = v * v
-        total = v[:, 0:128]
-        for j in range(1, v.shape[1] // 128):
-            total = total + v[:, j * 128 : (j + 1) * 128]
-        return total
-
-    rt = 64
-
-    def project(src, b, dst, out, gain, w, sq, depth, kt):
-        rows = src.shape[1]
+    ones = jnp.ones((512, 128), jnp.bfloat16)
+
+    def project(src, b, in_place, out, gain, w, sq):
+        kt = ones.shape[0]
         sq[...] = jnp.zeros_like(sq)
         out[...] = jnp.zeros_like(out)
-
-        @pl.loop(0, depth // kt)
+        rows = src.shape[1]
+
+        @pl.loop(0, src.shape[2] // kt)
         def _(k):
             ks = pl.ds(pl.multiple_of(k * kt, kt), kt)
-            gain_k = gain[:, ks]
-
-            @pl.loop(0, rows // rt)
-            def _(i):
-                rs = pl.ds(pl.multiple_of(i * rt, rt), rt)
-                v = src[b, rs, ks].astype(jnp.float32)
-                sq[rs, :] += square_lanes(v)
-                if dst is None:
-                    src[b, rs, ks] = (v * gain_k).astype(jnp.bfloat16)
-                else:
-                    dst[rs, :] = (v * gain_k).astype(jnp.bfloat16)
-
-            gated = src[b, :, ks] if dst is None else dst[...]
+            v = src[b, :, ks].astype(jnp.float32)
+            lanes = [gain[pl.ds(k * (kt // 128) + j, 1), :] for j in range(kt // 128)]
+            gated = (v * jnp.concatenate(lanes, axis=1)).astype(jnp.bfloat16)
+            if in_place:
+                src[b, :, ks] = gated
             out[...] += jnp.dot(gated, w[ks, :], preferred_element_type=jnp.float32)
-
-    def send_half(out, stage_out, stage_in, sq, q_out, q_in, slot):
+            sq[0:rows, :] += jnp.dot(
+                (v * v).astype(jnp.bfloat16), ones, preferred_element_type=jnp.float32
+            )
+
+    def stage(out, stage_out, sq, q_out, slot):
         stage_out[slot] = out[:, give].astype(jnp.bfloat16)
         q_out[slot] = jnp.broadcast_to(
-            jnp.sum(sq[...].T, axis=0, keepdims=True), q_out.shape[1:]
+            sq[...].T[0:1], q_out.shape[1:]
         )
-        return stage_out, q_out
 
     def x_pair(stage_out, stage_in, q_out, q_in, slot, n):
         return (
@@ -190,10 +181,13 @@
         if step == 0:
             loc[0].wait()
             loc[1].wait()
+            loc[2].start()
+            loc[3].start()
+            sib_x.start()
         else:
             sib_t.wait_recv()
-        project(tr, b, gt, tp.at[step], tg_ref, tw, tsq, tk, 512)
-        send_half(tp.at[step], tx_out, tx_in, tsq, tq_out, tq_in, step)
+        project(tr, b, False, tp.at[step], tg_ref, tw, tsq)
+        stage(tp.at[step], tx_out, tsq, tq_out, step)
         pair = x_pair(tx_out, tx_in, tq_out, tq_in, step, step)
         for c in pair:
             c.start()
@@ -208,22 +202,35 @@
             loc[3].wait()
         else:
             sib_x.wait_recv()
-        project(sr, b, None, sp.at[step], sg_ref, sw, ssq, sk, 512)
-        send_half(sp.at[step], sx_out, sx_in, ssq, sq_out, sq_in, step)
-        pair = x_pair(sx_out, sx_in, sq_out, sq_in, step, 2 + step)
-        for c in pair:
+        project(sr, b, True, sp.at[step], sg_ref, sw, ssq)
+        for sub in range(2):
+            spot = pl.ds(pl.multiple_of((1 - x) * half + sub * 128, 128), 128)
+            sx_out[step, sub] = sp[step, :, spot].astype(jnp.bfloat16)
+        sq_out[step] = jnp.broadcast_to(ssq[...].T[0:1], sq_out.shape[1:])
+        q = remote(sq_out.at[step], sq_in.at[step], q_s.at[2 + step], q_r.at[2 + step], xp)
+        subs = [
+            remote(
+                sx_out.at[step, sub], sx_in.at[step, sub],
+                x_s.at[2 + 2 * step + sub], x_r.at[2 + 2 * step + sub], xp,
+            )
+            for sub in range(2)
+        ]
+        for c in [q] + subs:
             c.start()
-        s_copies.append(pair)
+        s_copies.append([q] + subs)
+
+        @pl.loop(0, n_f)
+        def _(f):
+            fs = pl.ds(pl.multiple_of(f * fb, fb), fb)
+            srt[b, fs, :] = sr[b, :, fs].T
 
     def column(row):
         n = row.shape[1]
         return jnp.broadcast_to(row, (128, n)).T
 
-    student(0)
-    loc[4].wait()
     sib_o.wait_recv()
     n_own = 2 * n_mp
-    wide = ow.shape[2]
+    z_copies = []
     for step in range(2):
         for c in t_copies[step]:
             c.wait_recv()
@@ -234,7 +241,8 @@
         values = tp[step, :, keep] + tx_in[step].astype(jnp.float32)
         values = (values * scale).astype(jnp.bfloat16)
         own = ow[b]
-        eq = (own == lax.broadcasted_iota(jnp.int32, (8, wide), 0)).astype(jnp.float32)
+        row_id = lax.broadcasted_iota(jnp.int32, (8, wide), 0).astype(jnp.float32)
+        eq = (own == row_id).astype(jnp.float32)
         upper = (
             lax.broadcasted_iota(jnp.int32, (wide, wide), 0)
             < lax.broadcasted_iota(jnp.int32, (wide, wide), 1)
@@ -243,7 +251,7 @@
             eq.astype(jnp.bfloat16), upper.astype(jnp.bfloat16), preferred_element_type=jnp.float32
         )
         rank = jnp.sum(eq * before, axis=0, keepdims=True)
-        dest = own[0:1, :].astype(jnp.float32) * cap + rank
+        dest = own[0:1, :] * cap + rank
         for o in range(n_own // 2):
             spot = lax.broadcasted_iota(jnp.int32, (2 * cap, wide), 0) + o * 2 * cap
             hit = (spot.astype(jnp.float32) == dest).astype(jnp.float32)
@@ -254,50 +262,57 @@
             moved = jnp.where(filled > 0.5, moved, SENTINEL).astype(jnp.bfloat16)
             pk[2 * o, b] = moved[0:cap]
             pk[2 * o + 1, b] = moved[cap:]
-    z_copies = []
-    for k in range(1, n_mp):
-        to = lax.rem(m + k, n_mp)
-        c = remote(pk.at[pl.ds(2 * to, 2)], tgt.at[:, m], z_s.at[k - 1], z_r.at[k - 1], z_dev(k))
-        c.start()
-        z_copies.append(c)
-    tgt[0, m] = pk[2 * m]
-    tgt[1, m] = pk[2 * m + 1]
+        for k in range(1, n_mp):
+            to = lax.rem(m + k, n_mp)
+            n = step * (n_mp - 1) + k - 1
+            c = remote(
+                pk.at[pl.ds(2 * to, 2), b], tgt.at[:, m, b], z_s.at[n], z_r.at[n], z_dev(k)
+            )
+            c.start()
+            z_copies.append(c)
+        tgt[0, m, b] = pk[2 * m, b]
+        tgt[1, m, b] = pk[2 * m + 1, b]
+        if step == 0:
+            student(0)
 
     student(1)
-    for step in range(2):
-        for c in s_copies[step]:
-            c.wait_recv()
     for c in z_copies:
         c.wait_recv()
 
     norm = 1.0 / math.sqrt(tokens)
     gap_copies = []
-    for step in range(2):
-        b = r if step == 0 else 1 - r
-        sq_sum = sq_out[step, 0:1, :] + sq_in[step, 0:1, :]
-        scale = column(lax.rsqrt(sq_sum / DS + EPS))
-        per = 2 * cap
-        for s in range(n_mp):
-            rs = slice(s * per, (s + 1) * per)
-            sc = jnp.concatenate([scale[rs]] * (half // 128), axis=1)
-            vals = (sp[step, rs, keep] + sx_in[step, rs].astype(jnp.float32)) * sc
-            target = tgt[b, s].reshape(per, half).astype(jnp.float32)
-            diff = jnp.where(target < 0.5 * SENTINEL, vals - target, 0.0)
-            gap_half[b, rs] = diff.astype(jnp.bfloat16)
-            cot[b, rs] = (diff * sc * norm).astype(jnp.bfloat16)
-        c = remote(gap_half.at[b], gap.at[b], g_s.at[step], g_r.at[step], xp)
-        c.start()
-        gap_copies.append(c)
-        sp[step, :, 0:128] = scale
-
-    fb = 256
-    n_f = sk // fb
+
+    def close_gap(sub):
+        spot = pl.ds(pl.multiple_of(x * half + sub * 128, 128), 128)
+        for step in range(2):
+            b = r if step == 0 else 1 - r
+            s_copies[step][1 + sub].wait_recv()
+            if sub == 0:
+                s_copies[step][0].wait_recv()
+                sq_sum = sq_out[step, 0:1, :] + sq_in[step, 0:1, :]
+                sc_ref[b] = column(lax.rsqrt(sq_sum / DS + EPS))
+            per = 2 * cap
+            for k in range(n_mp):
+                rs = slice(k * per, (k + 1) * per)
+                sc = sc_ref[b, rs]
+                vals = (sp[step, rs, spot] + sx_in[step, sub, rs].astype(jnp.float32)) * sc
+                target = tgt[b, k, :, :, sub * 128 : sub * 128 + 128].reshape(per, 128)
+                target = target.astype(jnp.float32)
+                diff = jnp.where(target < 0.5 * SENTINEL, vals - target, 0.0)
+                gap_half[sub, b, rs] = diff.astype(jnp.bfloat16)
+                cot[sub, b, rs] = (diff * sc * norm).astype(jnp.bfloat16)
+            n = 2 * sub + step
+            c = remote(gap_half.at[sub, b], gap.at[sub, b], g_s.at[n], g_r.at[n], xp)
+            c.start()
+            gap_copies.append(c)
+
     outer = (m == 0) | (m == n_mp - 1)
     inward = jnp.where(m < n_mp // 2, m + 1, m - 1)
     outward = jnp.where(m < n_mp // 2, m - 1, m + 1)
     near = (g, jnp.where(outer, inward, outward), r, x)
     across = (g, inward, r, x)
-    n_c = 2 * n_f
+    n_c = 4 * n_f
+    lag = 3
 
     def up(i):
         return remote(part_out.at[i], outer_in.at[i], a_s.at[i], a_r.at[i], near)
@@ -307,10 +322,11 @@
 
     def place(i):
         f = lax.rem(i, n_f)
-        h = jnp.where(i < n_f, x, 1 - x)
+        phase = i // n_f
+        h = jnp.where(phase < 2, x, 1 - x)
         return (
             pl.ds(pl.multiple_of(f * fb, fb), fb),
-            pl.ds(pl.multiple_of(h * half, half), half),
+            pl.ds(pl.multiple_of(h * half + lax.rem(phase, 2) * 128, 128), 128),
         )
 
     def down(i):
@@ -322,9 +338,7 @@
         fs = pl.ds(pl.multiple_of(f * fb, fb), fb)
         total = None
         for b in range(2):
-            term = lax.dot_general(
-                sr[b, :, fs], cot[b], (((0,), (0,)), ((), ())), preferred_element_type=jnp.float32
-            )
+            term = jnp.dot(srt[b, fs, :], cot[i // n_f, b], preferred_element_type=jnp.float32)
             total = term if total is None else total + term
         return total
 
@@ -348,29 +362,41 @@
             part_out[i] = (mine + outer_in[i].astype(jnp.float32)).astype(jnp.bfloat16)
             cross(i).start()
 
-            @pl.when(i > 0)
+            @pl.when(i >= lag)
             def _():
-                finish(i - 1)
+                finish(i - lag)
+
+    def error_spot(n):
+        h = x if n < 2 else 1 - x
+        return pl.ds(pl.multiple_of(h * half + (n % 2) * 128, 128), 128)
+
+    def error_from(n, b):
+        return (gap_half if n < 2 else gap).at[n % 2, b]
 
     def error_copy(n):
-        src, spot = (gap_half, keep) if n == 0 else (gap, give)
-        return remote(src.at[1 - r], err_ref.at[:, spot], v_s.at[n], v_r.at[n], sib)
-
-    pl.loop(0, n_f)(chunk)
-    for step in range(2):
-        b = r if step == 0 else 1 - r
-        gap_copies[step].wait_recv()
-        sc = jnp.concatenate([sp[step, :, 0:128]] * (half // 128), axis=1)
-        cot[b] = (gap[b].astype(jnp.float32) * sc * norm).astype(jnp.bfloat16)
+        return remote(
+            error_from(n, 1 - r), err_ref.at[:, error_spot(n)], v_s.at[n], v_r.at[n], sib
+        )
+
+    close_gap(0)
+    pl.loop(0, 4)(chunk)
+    close_gap(1)
+    pl.loop(4, 2 * n_f)(chunk)
+    for c in gap_copies:
+        c.wait_recv()
+    for sub in range(2):
+        for b in range(2):
+            cot[2 + sub, b] = (
+                gap[sub, b].astype(jnp.float32) * sc_ref[b] * norm
+            ).astype(jnp.bfloat16)
 
     @pl.when(r == x)
     def _():
-        error_copy(0).start()
-        error_copy(1).start()
-        err_ref[:, keep] = gap_half[r]
-        err_ref[:, give] = gap[r]
-
-    pl.loop(n_f, n_c)(chunk)
+        for n in range(4):
+            error_copy(n).start()
+            err_ref[:, error_spot(n)] = error_from(n, r)[...]
+
+    pl.loop(2 * n_f, n_c)(chunk)
 
     @pl.when(outer)
     def _():
@@ -381,7 +407,7 @@
 
     @pl.when(jnp.logical_not(outer))
     def _():
-        finish(n_c - 1)
+        pl.loop(n_c - lag, n_c)(finish)
 
         @pl.loop(0, n_c)
         def _(i):
@@ -390,13 +416,13 @@
 
     @pl.when(r == x)
     def _():
-        error_copy(0).wait_send()
-        error_copy(1).wait_send()
+        for n in range(4):
+            error_copy(n).wait_send()
 
     @pl.when(r != x)
     def _():
-        error_copy(0).wait_recv()
-        error_copy(1).wait_recv()
+        for n in range(4):
+            error_copy(n).wait_recv()
 
     for c in [sib_t, sib_o, sib_x] + z_copies + gap_copies:
         c.wait_send()
@@ -415,9 +441,7 @@
     n_mp = lax.axis_size("mp")
     cap = slots // (2 * n_mp)
     wide = -(-blk // 128) * 128
-    own = jnp.pad(owners[:, 0], (0, wide - blk), constant_values=-1)
-    own = jnp.broadcast_to(own[None, :], (8, wide))
-    n_c = 2 * (sk // 256)
+    n_c = 4 * (sk // 256)
     bf, f32, vmem, dma = jnp.bfloat16, jnp.float32, pltpu.VMEM, pltpu.SemaphoreType.DMA
     hbm = pl.BlockSpec(memory_space=pl.ANY)
     inv = pl.BlockSpec(memory_space=vmem)
@@ -426,35 +450,36 @@
         vmem((2, slots, sk), bf),
         vmem((tk, cols), bf),
         vmem((sk, cols), bf),
-        vmem((2, 8, wide), jnp.int32),
-        vmem((blk, 512), bf),
+        vmem((2, 8, wide), f32),
+        vmem((2, sk, slots), bf),
         vmem((2, blk, cols), f32),
         vmem((2, slots, cols), f32),
         vmem((wide, 128), f32),
         vmem((slots, 128), f32),
         vmem((2, blk, half), bf),
         vmem((2, blk, half), bf),
-        vmem((2, slots, half), bf),
-        vmem((2, slots, half), bf),
+        vmem((2, 2, slots, 128), bf),
+        vmem((2, 2, slots, 128), bf),
         vmem((2, 8, wide), f32),
         vmem((2, 8, wide), f32),
         vmem((2, 8, slots), f32),
         vmem((2, 8, slots), f32),
         vmem((2 * n_mp, 2, cap, half), bf),
         vmem((2, n_mp, 2, cap, half), bf),
-        vmem((2, slots, half), bf),
-        vmem((2, slots, half), bf),
-        vmem((2, slots, half), bf),
-        vmem((n_c, 256, half), bf),
-        vmem((n_c, 256, half), bf),
-        vmem((n_c, 256, half), bf),
-        dma((5,)),
+        vmem((2, 2, slots, 128), bf),
+        vmem((2, 2, slots, 128), bf),
+        vmem((4, 2, slots, 128), bf),
+        vmem((2, slots, 128), f32),
+        vmem((n_c, 256, 128), bf),
+        vmem((n_c, 256, 128), bf),
+        vmem((n_c, 256, 128), bf),
+        dma((4,)),
         dma((3,)), dma((3,)),
+        dma((6,)), dma((6,)),
+        dma((4,)), dma((4,)),
+        dma((2 * n_mp - 2,)), dma((2 * n_mp - 2,)),
         dma((4,)), dma((4,)),
         dma((4,)), dma((4,)),
-        dma((3,)), dma((3,)),
-        dma((2,)), dma((2,)),
-        dma((2,)), dma((2,)),
         dma((n_c,)), dma((n_c,)),
         dma((n_c,)), dma((n_c,)),
         dma((n_c,)), dma((n_c,)),
@@ -465,7 +490,7 @@
             jax.ShapeDtypeStruct((slots, cols), bf),
             jax.ShapeDtypeStruct((sk, cols), bf),
         ),
-        in_specs=[hbm, inv, hbm, hbm, inv, hbm, hbm],
+        in_specs=[hbm, inv, hbm, hbm, inv, hbm, inv],
         out_specs=(inv, inv),
         scratch_shapes=scratch,
         compiler_params=pltpu.CompilerParams(
@@ -475,8 +500,8 @@
             flops=10 * 10**9, bytes_accessed=20 * 10**6, transcendentals=0
         ),
     )(
-        teacher_rows, teacher_gain[None, :], teacher_value,
-        student_rows, student_gain[None, :], student_value, own,
+        teacher_rows, teacher_gain.reshape(-1, 128), teacher_value,
+        student_rows, student_gain.reshape(-1, 128), student_value, owners.reshape(1, blk),
     )
     return err, grad.astype(f32)
 

time: 118 us -> 110 us (0.932)
  Pallas kernels: 109 us -> 104 us
  local copies, waits for them, and re-layouts: 2.76 us -> 0.84 us
    pallas_call x1, Pallas kernels: 109 us -> 104 us  [shards_fused(): pl.pallas_call(fused, out_shape=(jax.ShapeDtypeStruct((slots, cols), bf),...]
    broadcast_in_dim x2 -> x0, local copies, waits for them, and re-layouts: 1.91 us -> none  [the longest x1 1.31 us: shards_fused(): student_gain[None, :]]
where the time goes in v2:
time: 110 us
  Pallas kernels  104 us (95%)
  other arithmetic  4.91 us (4%)
    pallas_call x1, Pallas kernels, shards_fused(): pl.pallas_call(fused, out_shape=(jax.ShapeDtypeStruct((slots, cols), bf),...  104 us
    convert_element_type x1, other arithmetic, shards_fused(): return (err, grad.astype(f32))  4.91 us

profile of v2, /device:TPU:0, one launch (start us, length us, event | category | flops | bytes accessed | tf_op | source)
XLA Modules:
  0.0 110.1 jit_solution(12659656199950322142)
XLA Ops:
  0.6 103.7 %shard_map.86 = (bf16[640,512]{1,0:T(8,128)(2,1)}, bf16[2560,512]{1,0:T(8,128)(2,1)}) custom-call(bf16[320,4096]{1,0:T(8,128)(2,1)} %t_hbm.1, f32[32,128]{1,0:T(8,128)} %bitcast.3, bf16[4096,512]{1,0:T(8,128)(2,1)} %tw_hbm.1, bf16[640,2560]{1,0:T(8,128)(2,1)} %s_hbm.1, f32[20,128]{1,0:T(8,128)} %bitcast.4, bf16[2560,512]{1,0:T(8,128)(2,1)} %sw_hbm.1, ...), custom_call_target="tpu_custom_call" | custom-call | flops 10000000000 | bytes 20000000 | tf_op jit(solution)/shard_map/pallas_call | solution.py:487
  104.3 0.0 copy-start
  104.3 4.9 %convert_element_type.3 = f32[2560,512]{1,0:T(8,128)} convert(bf16[2560,512]{1,0:T(8,128)(2,1)} %get-tuple-element.5) | non-fusion elementwise | flops 1310720 | bytes 7864320 | tf_op jit(solution)/shard_map/convert_element_type | solution.py:506
  109.2 0.0 copy-done
  109.2 0.8 copy.10
Async XLA Ops:
  104.3 4.9 %copy-start = (bf16[640,512]{1,0:T(8,128)(2,1)S(1)}, bf16[640,512]{1,0:T(8,128)(2,1)}, u32[]{:S(2)}) copy-start(bf16[640,512]{1,0:T(8,128)(2,1)} %get-tuple-element.8) | copy-start | bytes 1966084

commit v3 on v2

--- a/solution.py
+++ b/solution.py
@@ -218,11 +218,6 @@
         for c in [q] + subs:
             c.start()
         s_copies.append([q] + subs)
-
-        @pl.loop(0, n_f)
-        def _(f):
-            fs = pl.ds(pl.multiple_of(f * fb, fb), fb)
-            srt[b, fs, :] = sr[b, :, fs].T
 
     def column(row):
         n = row.shape[1]
@@ -276,6 +271,13 @@
             student(0)
 
     student(1)
+
+    @pl.loop(0, n_f)
+    def _(f):
+        fs = pl.ds(pl.multiple_of(f * fb, fb), fb)
+        for b in range(2):
+            srt[b, fs, :] = sr[b, :, fs].T
+
     for c in z_copies:
         c.wait_recv()
 

time: 110 us -> 110 us (level)
  no operation moved by 1% of the time
where the time goes in v3:
time: 110 us
  Pallas kernels  104 us (95%)
  other arithmetic  4.91 us (4%)
    pallas_call x1, Pallas kernels, shards_fused(): pl.pallas_call(fused, out_shape=(jax.ShapeDtypeStruct((slots, cols), bf),...  104 us
    convert_element_type x1, other arithmetic, shards_fused(): return (err, grad.astype(f32))  4.91 us

profile of v3, /device:TPU:0, one launch (start us, length us, event | category | flops | bytes accessed | tf_op | source)
XLA Modules:
  0.0 110.1 jit_solution(18381507647504256357)
XLA Ops:
  0.6 103.7 %shard_map.86 = (bf16[640,512]{1,0:T(8,128)(2,1)}, bf16[2560,512]{1,0:T(8,128)(2,1)}) custom-call(bf16[320,4096]{1,0:T(8,128)(2,1)} %t_hbm.1, f32[32,128]{1,0:T(8,128)} %bitcast.3, bf16[4096,512]{1,0:T(8,128)(2,1)} %tw_hbm.1, bf16[640,2560]{1,0:T(8,128)(2,1)} %s_hbm.1, f32[20,128]{1,0:T(8,128)} %bitcast.4, bf16[2560,512]{1,0:T(8,128)(2,1)} %sw_hbm.1, ...), custom_call_target="tpu_custom_call" | custom-call | flops 10000000000 | bytes 20000000 | tf_op jit(solution)/shard_map/pallas_call | solution.py:489
  104.3 0.0 copy-start
  104.3 4.9 %convert_element_type.3 = f32[2560,512]{1,0:T(8,128)} convert(bf16[2560,512]{1,0:T(8,128)(2,1)} %get-tuple-element.5) | non-fusion elementwise | flops 1310720 | bytes 7864320 | tf_op jit(solution)/shard_map/convert_element_type | solution.py:508
  109.2 0.0 copy-done
  109.2 0.8 copy.10
Async XLA Ops:
  104.3 4.9 %copy-start = (bf16[640,512]{1,0:T(8,128)(2,1)S(1)}, bf16[640,512]{1,0:T(8,128)(2,1)}, u32[]{:S(2)}) copy-start(bf16[640,512]{1,0:T(8,128)(2,1)} %get-tuple-element.8) | copy-start | bytes 1966084
